TPU v7x, 256 devices: a whole 4x4x8 slice. The times are simulated.
256 devices in a mesh: leaf: 16 (over z, core), row: 4 (over y), col: 4 (over x).
Axes of the slice: x: 4, y: 4, z: 8, core: 2. Of those that a mesh axis runs over, the one named last changes fastest.
Arguments:
- sketch_leaf: bfloat16 [131072, 256], P(('leaf', 'row'), 'col'), may hold values from -6 to 6
- sketch_sep: bfloat16 [8192, 256], P(('row', 'col')), may hold values from -6 to 6
- leaf_inverse: bfloat16 [131072, 8192], P(('leaf', 'col'), 'row'), as said below
- coupling: bfloat16 [131072, 2048], P(('leaf', 'col'), 'row'), may hold values from -0.0625 to 0.0625
- sep_inverse: bfloat16 [8192, 8192], P('leaf', ('row', 'col'))
- front_map: int32 [16, 16], replicated, may hold values from 0 to 63, as said below
Outputs:
- sketch_out_leaf: float32 [131072, 256], P(('leaf', 'row'), 'col')
- sketch_out_sep: float32 [8192, 256], P(('row', 'col'))
Inputs may be any that keep to these rules, and one draw needn't show every extreme that they name: `front_map`: row block q of every section's coupling lies in separator blocks q * 4 to q * 4 + 3. leaf_inverse and sep_inverse are inverses of lower triangular factor blocks (in natural order), stored in block-cyclic order.
All inputs are finite; a program needn't handle non-finite values.
Results may differ from a plain program's by a relative error of at most 0.024.
Values may be sent and summed in bfloat16 or wider, within the bound.
A program may use at most 64 MiB of HBM per device.

v0:
```python
import jax
import jax.numpy as jnp
from jax import lax
from jax.sharding import PartitionSpec as P


def contract_rows(left, right):
    return lax.dot_general(
        left, right, (((0,), (0,)), ((), ())), preferred_element_type=jnp.float32
    )


def shards(sketch_leaf, sketch_sep, leaf_inverse, coupling, sep_inverse, front_map):
    columns = sketch_leaf.shape[1] * lax.axis_size("col")
    q_index = lax.axis_index("row") * lax.axis_size("col") + lax.axis_index("col")
    section = lax.axis_index("leaf")
    partial_value = jnp.dot(
        leaf_inverse,
        lax.all_gather(sketch_leaf, "col", axis=1, tiled=True),
        preferred_element_type=jnp.float32,
    )
    front_z = lax.psum_scatter(partial_value, "row", scatter_dimension=1, tiled=True).astype(
        jnp.bfloat16
    )
    coupled_part = contract_rows(coupling, lax.all_gather(front_z, "row", axis=1, tiled=True))
    coupled = lax.psum_scatter(coupled_part, "col", scatter_dimension=0, tiled=True).astype(
        jnp.bfloat16
    )
    block_rows = coupled.shape[0]
    group = sketch_sep.shape[0] // block_rows
    own_slot = front_map[section, q_index] - q_index * group
    place = (jnp.arange(group, dtype=jnp.int32) == own_slot).astype(jnp.float32)
    spread = (place[:, None, None] * coupled.astype(jnp.float32)[None]).reshape(
        group * block_rows, columns
    )
    total = lax.psum(spread.astype(jnp.bfloat16), "leaf").astype(jnp.float32)
    sep_rhs = (sketch_sep.astype(jnp.float32) - total).astype(jnp.bfloat16)
    sep_part = jnp.dot(sep_inverse, sep_rhs, preferred_element_type=jnp.float32)
    sep_mid = lax.psum(sep_part.astype(jnp.bfloat16), ("row", "col"))
    sketch_out_sep = lax.psum(
        contract_rows(sep_inverse, sep_mid).astype(jnp.bfloat16), "leaf"
    ).astype(jnp.float32)
    sep_round = sketch_out_sep.astype(jnp.bfloat16)
    pulled = lax.dynamic_slice_in_dim(sep_round, own_slot * block_rows, block_rows, 0)
    back_part = jnp.dot(
        coupling,
        lax.all_gather(pulled, "col", axis=0, tiled=True),
        preferred_element_type=jnp.float32,
    )
    back_slice = lax.psum_scatter(
        back_part.astype(jnp.bfloat16), "row", scatter_dimension=1, tiled=True
    ).astype(jnp.float32)
    leaf_rhs = (front_z.astype(jnp.float32) - back_slice).astype(jnp.bfloat16)
    out_part = contract_rows(leaf_inverse, lax.all_gather(leaf_rhs, "row", axis=1, tiled=True))
    sketch_out_leaf = lax.psum_scatter(
        out_part.astype(jnp.bfloat16), "col", scatter_dimension=1, tiled=True
    ).astype(jnp.float32)
    return (sketch_out_leaf, sketch_out_sep)


def solution(mesh):
    placed = (
        P(("leaf", "row"), "col"),
        P(("row", "col"), None),
        P(("leaf", "col"), "row"),
        P(("leaf", "col"), "row"),
        P("leaf", ("row", "col")),
        P(),
    )
    return jax.shard_map(
        shards,
        mesh=mesh,
        in_specs=placed,
        out_specs=(P(("leaf", "row"), "col"), P(("row", "col"), None)),
        check_vma=False,
    )
```

profile of v0, /device:TPU:8, one launch (start us, length us, event | category | flops | bytes accessed | tf_op | source)
XLA Modules:
  0.0 567.1 jit_solution(8834700790642962263)
XLA Ops:
  7.2 0.0 copy-start
  7.2 0.0 all-gather.4.cloned.1.call-start
  7.2 0.7 all-gather.4.cloned.1.call-update
  7.9 0.0 reduce-scatter.5.cloned.1.call-start
  8.0 31.3 %all-gather.4.cloned.1.call-done = bf16[2048,256]{0,1:T(8,128)(2,1)} async-done(((bf16[2048,64]{0,1:T(8,128)(2,1)}), bf16[2048,256]{0,1:T(8,128)(2,1)}) %all-gather.4.cloned.1.call-update) | async-done | bytes 1048592 | tf_op jit(solution)/shard_map/all_gather | solution.py:19
  39.2 7.3 %fusion.5 = f32[2048,256]{0,1:T(8,128)} fusion(bf16[2048,2048]{1,0:T(8,128)(2,1)} %param.8, bf16[2048,256]{0,1:T(8,128)(2,1)} %all-gather.4.cloned.1.call-done), kind=kOutput, calls=%fused_computation.17 | convolution fusion | flops 2147483648 | bytes 11534336 | tf_op jit(solution)/shard_map/dot_general | solution.py:17
  46.5 0.0 reduce-scatter.5.cloned.1.call-update
  46.6 0.0 all-gather.6.cloned.1.call-start
  46.6 31.5 %reduce-scatter.5.cloned.1.call-done = f32[2048,64]{0,1:T(8,128)} async-done(((f32[2048,256]{0,1:T(8,128)}), f32[2048,64]{0,1:T(8,128)}) %reduce-scatter.5.cloned.1.call-update) | async-done | bytes 524304 | tf_op jit(solution)/shard_map/reduce_scatter | solution.py:22
  78.1 1.8 convert_element_type.68
  79.9 0.0 all-gather.6.cloned.1.call-update
  79.9 0.0 copy-start.1
  79.9 0.0 copy-start.4
  79.9 0.0 reduce-scatter.7.cloned.1.call-start
  80.0 27.3 %all-gather.6.cloned.1.call-done = bf16[2048,256]{0,1:T(8,128)(2,1)} async-done(((bf16[2048,64]{0,1:T(8,128)(2,1)}), bf16[2048,256]{0,1:T(8,128)(2,1)}) %all-gather.6.cloned.1.call-update) | async-done | bytes 1048592 | tf_op jit(solution)/shard_map/all_gather | solution.py:25
  107.2 0.0 copy-done
  107.3 2.7 convolution_bitcast_fusion
  110.0 0.0 reduce-scatter.7.cloned.1.call-update
  110.0 0.0 all-reduce.4.cloned.1.call-start
  110.1 1.3 dynamic_slice.6
  112.0 0.1 broadcast_bitcast_fusion
  112.1 23.5 %reduce-scatter.7.cloned.1.call-done = f32[128,256]{0,1:T(8,128)} async-done(((f32[512,256]{0,1:T(8,128)}), f32[128,256]{0,1:T(8,128)}) %reduce-scatter.7.cloned.1.call-update) | async-done | bytes 131088 | tf_op jit(solution)/shard_map/reduce_scatter | solution.py:26
  135.6 0.9 convert_convert_fusion
  136.5 0.1 copy.8
  136.6 0.8 fusion.4
  137.4 0.0 all-reduce.4.cloned.1.call-update
  137.5 0.0 all-reduce.6.cloned.1.call-start
  137.5 109.2 %all-reduce.4.cloned.1.call-done = bf16[512,256]{1,0:T(8,128)(2,1)} async-done(((bf16[512,256]{1,0:T(8,128)(2,1)}), bf16[512,256]{1,0:T(8,128)(2,1)}) %all-reduce.4.cloned.1.call-update) | async-done | bytes 262160 | tf_op jit(solution)/shard_map/psum | solution.py:36
  246.7 0.0 copy-done.1
  246.7 0.0 copy-done.4
  246.7 2.0 fusion.2
  248.7 0.0 all-reduce.6.cloned.1.call-update
  248.7 0.0 all-reduce.8.cloned.1.call-start
  248.8 95.9 %all-reduce.6.cloned.1.call-done = bf16[512,256]{0,1:T(8,128)(2,1)} async-done(((bf16[512,256]{0,1:T(8,128)(2,1)}), bf16[512,256]{0,1:T(8,128)(2,1)}) %all-reduce.6.cloned.1.call-update) | async-done | bytes 262160 | tf_op jit(solution)/shard_map/psum | solution.py:39
  344.7 2.0 fusion.3
  346.6 0.0 all-reduce.8.cloned.1.call-update
  346.7 0.0 reduce-scatter.9.cloned.1.call-start
  346.7 109.1 %all-reduce.8.cloned.1.call-done = bf16[512,256]{0,1:T(8,128)(2,1)} async-done(((bf16[512,256]{0,1:T(8,128)(2,1)}), bf16[512,256]{0,1:T(8,128)(2,1)}) %all-reduce.8.cloned.1.call-update) | async-done | bytes 262160 | tf_op jit(solution)/shard_map/psum | solution.py:40
  455.8 0.8 constant_dynamic-slice_fusion
  456.7 12.0 %all_gather.14 = bf16[512,256]{0,1:T(8,128)(2,1)S(1)} all-gather(bf16[128,256]{0,1:T(8,128)(2,1)S(1)} %constant_dynamic-slice_fusion), channel_id=1, replica_groups=mesh['leaf'=16,'row'=4,'col'=4] {'col'}, dimensions={0}, use_global_device_ids=true | all-gather | bytes 327680 | tf_op jit(solution)/shard_map/all_gather | solution.py:47
  468.7 0.0 copy-start.2
  468.7 1.7 fusion.1
  470.4 0.0 reduce-scatter.9.cloned.1.call-update
  470.4 0.0 all-gather.8.cloned.1.call-start
  470.5 23.6 %reduce-scatter.9.cloned.1.call-done = bf16[2048,64]{0,1:T(8,128)(2,1)} async-done(((bf16[2048,256]{0,1:T(8,128)(2,1)}), bf16[2048,64]{0,1:T(8,128)(2,1)}) %reduce-scatter.9.cloned.1.call-update) | async-done | bytes 262160 | tf_op jit(solution)/shard_map/reduce_scatter | solution.py:50
  494.0 0.0 copy-done.2
  494.0 1.7 subtract_convert_fusion
  495.7 0.0 all-gather.8.cloned.1.call-update
  495.7 0.0 copy-start.3
  495.7 0.0 reduce-scatter.11.cloned.1.call-start
  495.8 28.2 %all-gather.8.cloned.1.call-done = bf16[2048,256]{0,1:T(8,128)(2,1)} async-done(((bf16[2048,64]{0,1:T(8,128)(2,1)}), bf16[2048,256]{0,1:T(8,128)(2,1)}) %all-gather.8.cloned.1.call-update) | async-done | bytes 1048592 | tf_op jit(solution)/shard_map/all_gather | solution.py:54
  524.0 7.0 %fusion = bf16[2048,256]{0,1:T(8,128)(2,1)} fusion(bf16[2048,256]{0,1:T(8,128)(2,1)} %all-gather.8.cloned.1.call-done, bf16[2048,2048]{1,0:T(8,128)(2,1)} %param.8), kind=kOutput, calls=%fused_computation.2 | convolution fusion | flops 2148007936 | bytes 10485760 | tf_op jit(solution)/shard_map/dot_general | solution.py:8
  531.0 0.0 reduce-scatter.11.cloned.1.call-update
  531.0 0.0 copy-done.3
  531.0 0.9 copy.9
  532.0 26.5 %reduce-scatter.11.cloned.1.call-done = bf16[2048,64]{0,1:T(8,128)(2,1)} async-done(((bf16[2048,256]{0,1:T(8,128)(2,1)}), bf16[2048,64]{0,1:T(8,128)(2,1)}) %reduce-scatter.11.cloned.1.call-update) | async-done | bytes 262160 | tf_op jit(solution)/shard_map/reduce_scatter | solution.py:55
  558.5 1.8 convert_element_type.87
  (1 shorter events, 0.0 us)
Async XLA Ops:
  7.2 100.1 %copy-start = (bf16[2048,512]{1,0:T(8,128)(2,1)S(1)}, bf16[2048,512]{1,0:T(8,128)(2,1)}, u32[]{:S(2)}) copy-start(bf16[2048,512]{1,0:T(8,128)(2,1)} %param.9) | copy-start | bytes 6291460
  7.2 32.1 %all-gather.4.cloned.1.call-start = ((), (), s32[]{:S(2)}) async-start(), calls=%async_computation.4 | async-start | bytes 1310720 | tf_op jit(solution)/shard_map/all_gather | solution.py:19
  7.9 70.2 %reduce-scatter.5.cloned.1.call-start = ((), (), s32[]{:S(2)}) async-start(), calls=%async_computation.5 | async-start | bytes 2621440 | tf_op jit(solution)/shard_map/reduce_scatter | solution.py:22
  46.6 60.7 %all-gather.6.cloned.1.call-start = ((), (), s32[]{:S(2)}) async-start(), calls=%async_computation.6 | async-start | bytes 1310720 | tf_op jit(solution)/shard_map/all_gather | solution.py:25
  79.9 166.8 %copy-start.1 = (bf16[512,512]{1,0:T(8,128)(2,1)S(1)}, bf16[512,512]{1,0:T(8,128)(2,1)}, u32[]{:S(2)}) copy-start(bf16[512,512]{1,0:T(8,128)(2,1)} %param.10) | copy-start | bytes 1572868
  79.9 166.8 %copy-start.4 = (bf16[512,256]{1,0:T(8,128)(2,1)S(1)}, bf16[512,256]{1,0:T(8,128)(2,1)}, u32[]{:S(2)}) copy-start(bf16[512,256]{1,0:T(8,128)(2,1)} %param.7) | copy-start | bytes 786436
  79.9 55.7 %reduce-scatter.7.cloned.1.call-start = ((), (), s32[]{:S(2)}) async-start(), calls=%async_computation.7 | async-start | bytes 655360 | tf_op jit(solution)/shard_map/reduce_scatter | solution.py:26
  110.0 136.7 %all-reduce.4.cloned.1.call-start = ((), (), s32[]{:S(2)}) async-start(), calls=%async_computation.8 | async-start | bytes 524288 | tf_op jit(solution)/shard_map/psum | solution.py:36
  137.5 207.2 %all-reduce.6.cloned.1.call-start = ((), (), s32[]{:S(2)}) async-start(), calls=%async_computation.9 | async-start | bytes 524288 | tf_op jit(solution)/shard_map/psum | solution.py:39
  248.7 207.1 %all-reduce.8.cloned.1.call-start = ((), (), s32[]{:S(2)}) async-start(), calls=%async_computation.10 | async-start | bytes 524288 | tf_op jit(solution)/shard_map/psum | solution.py:40
  346.7 147.3 %reduce-scatter.9.cloned.1.call-start = ((), (), s32[]{:S(2)}) async-start(), calls=%async_computation.11 | async-start | bytes 1310720 | tf_op jit(solution)/shard_map/reduce_scatter | solution.py:50
  468.7 25.4 %copy-start.2 = (f32[2048,64]{0,1:T(8,128)S(1)}, f32[2048,64]{0,1:T(8,128)}, u32[]{:S(2)}) copy-start(f32[2048,64]{0,1:T(8,128)} %reduce-scatter.5.cloned.1.call-done) | copy-start | bytes 1572868
  470.4 53.6 %all-gather.8.cloned.1.call-start = ((), (), s32[]{:S(2)}) async-start(), calls=%async_computation.12 | async-start | bytes 1310720 | tf_op jit(solution)/shard_map/all_gather | solution.py:54
  495.7 35.3 %copy-start.3 = (bf16[512,256]{0,1:T(8,128)(2,1)S(1)}, bf16[512,256]{0,1:T(8,128)(2,1)}, u32[]{:S(2)}) copy-start(bf16[512,256]{0,1:T(8,128)(2,1)} %all-reduce.8.cloned.1.call-done) | copy-start | bytes 786436
  495.7 62.8 %reduce-scatter.11.cloned.1.call-start = ((), (), s32[]{:S(2)}) async-start(), calls=%async_computation.13 | async-start | bytes 1310720 | tf_op jit(solution)/shard_map/reduce_scatter | solution.py:55
Sparse Core Ops, SparseCore 0:
  9.8 29.3 all-gather.3
  46.7 31.3 reduce-scatter.4
  80.6 26.5 all-gather.5
  110.4 25.1 reduce-scatter.6
  138.4 108.2 all-reduce.3
  250.3 94.3 all-reduce.5
  347.7 108.0 all-reduce.7
  470.5 23.4 reduce-scatter.8
  496.5 27.3 all-gather.7
  531.1 27.3 reduce-scatter.10
where the time goes:
time: 568 us; the launch traced here: 567 us
  waiting for transfers between devices  507 us (89%)
  matrix products  22.8 us (4%)
  between operations  14.9 us (3%)
  blocking collectives  12 us (2%)
  other arithmetic  7 us (1%)
    psum x1, waiting for transfers between devices, shards(): total = lax.psum(spread.astype(jnp.bfloat16), 'leaf').astype(jnp.float32)  109 us
    psum x1, waiting for transfers between devices, shards(): lax.psum(contract_rows(sep_inverse, sep_mid).astype(jnp.bfloat16), 'leaf')  109 us
    psum x1, waiting for transfers between devices, shards(): sep_mid = lax.psum(sep_part.astype(jnp.bfloat16), ('row', 'col'))  95.9 us
    reduce_scatter x1, waiting for transfers between devices, shards(): lax.psum_scatter(partial_value, 'row', scatter_dimension=1, tiled=True)  31.5 us
    all_gather x1, waiting for transfers between devices, shards(): lax.all_gather(sketch_leaf, 'col', axis=1, tiled=True)  31.3 us
    all_gather x1, waiting for transfers between devices, shards(): lax.all_gather(leaf_rhs, 'row', axis=1, tiled=True)  28.2 us
    all_gather x1, waiting for transfers between devices, shards(): lax.all_gather(front_z, 'row', axis=1, tiled=True)  27.3 us
    reduce_scatter x1, waiting for transfers between devices, shards(): lax.psum_scatter(out_part.astype(jnp.bfloat16), 'col', scatter_dimension=...  26.5 us
  transfers between devices with their start and end apart: 10, of which 10 were waited for; matrix products, arithmetic and copies ran while one was open for 0% of the time, Pallas kernels for 0%

commit v1 on v0

--- a/solution.py
+++ b/solution.py
@@ -2,6 +2,11 @@
 import jax.numpy as jnp
 from jax import lax
 from jax.sharding import PartitionSpec as P
+
+
+def summed_here(block, name):
+    parts = lax.all_gather(block, name)
+    return jnp.sum(parts, axis=0)
 
 
 def contract_rows(left, right):
@@ -36,7 +41,7 @@
     total = lax.psum(spread.astype(jnp.bfloat16), "leaf").astype(jnp.float32)
     sep_rhs = (sketch_sep.astype(jnp.float32) - total).astype(jnp.bfloat16)
     sep_part = jnp.dot(sep_inverse, sep_rhs, preferred_element_type=jnp.float32)
-    sep_mid = lax.psum(sep_part.astype(jnp.bfloat16), ("row", "col"))
+    sep_mid = summed_here(sep_part.astype(jnp.bfloat16), ("row", "col"))
     sketch_out_sep = lax.psum(
         contract_rows(sep_inverse, sep_mid).astype(jnp.bfloat16), "leaf"
     ).astype(jnp.float32)

time: 568 us -> 540 us (0.951)
  waiting for transfers between devices: 507 us -> 473 us
    psum x1 -> x0, waiting for transfers between devices: 95.9 us -> none  [shards(): sep_mid = lax.psum(sep_part.astype(jnp.bfloat16), ('row', 'col'))]
    all_gather x0 -> x1, waiting for transfers between devices: none -> 63.4 us  [summed_here(): parts = lax.all_gather(block, name)]
where the time goes in v1:
time: 540 us; the launch traced here: 539 us
  waiting for transfers between devices  473 us (88%)
  matrix products  21.8 us (4%)
  between operations  14.9 us (3%)
  blocking collectives  12 us (2%)
  other arithmetic  9.54 us (2%)
  local copies, waits for them, and re-layouts  7.29 us (1%)
    psum x1, waiting for transfers between devices, shards(): total = lax.psum(spread.astype(jnp.bfloat16), 'leaf').astype(jnp.float32)  109 us
    psum x1, waiting for transfers between devices, shards(): lax.psum(contract_rows(sep_inverse, sep_mid).astype(jnp.bfloat16), 'leaf')  108 us
    all_gather x1, waiting for transfers between devices, summed_here(): parts = lax.all_gather(block, name)  63.4 us
    reduce_scatter x1, waiting for transfers between devices, shards(): lax.psum_scatter(partial_value, 'row', scatter_dimension=1, tiled=True)  31.5 us
    all_gather x1, waiting for transfers between devices, shards(): lax.all_gather(sketch_leaf, 'col', axis=1, tiled=True)  31.3 us
    all_gather x1, waiting for transfers between devices, shards(): lax.all_gather(leaf_rhs, 'row', axis=1, tiled=True)  27.9 us
    all_gather x1, waiting for transfers between devices, shards(): lax.all_gather(front_z, 'row', axis=1, tiled=True)  27.3 us
    reduce_scatter x1, waiting for transfers between devices, shards(): lax.psum_scatter(out_part.astype(jnp.bfloat16), 'col', scatter_dimension=...  26.5 us
  transfers between devices with their start and end apart: 10, of which 10 were waited for; matrix products, arithmetic and copies ran while one was open for 0% of the time, Pallas kernels for 0%

profile of v1, /device:TPU:8, one launch (start us, length us, event | category | flops | bytes accessed | tf_op | source)
XLA Modules:
  0.0 539.2 jit_solution(5227489508755918257)
XLA Ops:
  7.2 0.0 copy-start
  7.2 0.0 all-gather.6.cloned.1.call-start
  7.2 0.7 all-gather.6.cloned.1.call-update
  7.9 0.0 reduce-scatter.5.cloned.1.call-start
  8.0 31.3 %all-gather.6.cloned.1.call-done = bf16[2048,256]{0,1:T(8,128)(2,1)} async-done(((bf16[2048,64]{0,1:T(8,128)(2,1)}), bf16[2048,256]{0,1:T(8,128)(2,1)}) %all-gather.6.cloned.1.call-update) | async-done | bytes 1048592 | tf_op jit(solution)/shard_map/all_gather | solution.py:24
  39.2 7.3 %fusion.5 = f32[2048,256]{0,1:T(8,128)} fusion(bf16[2048,2048]{1,0:T(8,128)(2,1)} %param.8, bf16[2048,256]{0,1:T(8,128)(2,1)} %all-gather.6.cloned.1.call-done), kind=kOutput, calls=%fused_computation.18 | convolution fusion | flops 2147483648 | bytes 11534336 | tf_op jit(solution)/shard_map/dot_general | solution.py:22
  46.5 0.0 reduce-scatter.5.cloned.1.call-update
  46.6 0.0 all-gather.8.cloned.1.call-start
  46.6 31.5 %reduce-scatter.5.cloned.1.call-done = f32[2048,64]{0,1:T(8,128)} async-done(((f32[2048,256]{0,1:T(8,128)}), f32[2048,64]{0,1:T(8,128)}) %reduce-scatter.5.cloned.1.call-update) | async-done | bytes 524304 | tf_op jit(solution)/shard_map/reduce_scatter | solution.py:27
  78.1 1.8 convert_element_type.70
  79.9 0.0 all-gather.8.cloned.1.call-update
  79.9 0.0 copy-start.1
  79.9 0.0 copy-start.4
  79.9 0.0 reduce-scatter.7.cloned.1.call-start
  80.0 27.3 %all-gather.8.cloned.1.call-done = bf16[2048,256]{0,1:T(8,128)(2,1)} async-done(((bf16[2048,64]{0,1:T(8,128)(2,1)}), bf16[2048,256]{0,1:T(8,128)(2,1)}) %all-gather.8.cloned.1.call-update) | async-done | bytes 1048592 | tf_op jit(solution)/shard_map/all_gather | solution.py:30
  107.2 0.0 copy-done
  107.3 2.7 convolution_bitcast_fusion
  110.0 0.0 reduce-scatter.7.cloned.1.call-update
  110.0 0.0 all-reduce.3.cloned.1.call-start
  110.1 1.3 dynamic_slice.6
  112.0 0.1 broadcast_bitcast_fusion
  112.1 23.5 %reduce-scatter.7.cloned.1.call-done = f32[128,256]{0,1:T(8,128)} async-done(((f32[512,256]{0,1:T(8,128)}), f32[128,256]{0,1:T(8,128)}) %reduce-scatter.7.cloned.1.call-update) | async-done | bytes 131088 | tf_op jit(solution)/shard_map/reduce_scatter | solution.py:31
  135.6 0.9 convert_convert_fusion
  136.5 0.1 copy.10
  136.6 0.8 fusion.4
  137.4 0.0 all-reduce.3.cloned.1.call-update
  137.5 0.0 all-gather.12.cloned.1.call-start
  137.5 109.2 %all-reduce.3.cloned.1.call-done = bf16[512,256]{1,0:T(8,128)(2,1)} async-done(((bf16[512,256]{1,0:T(8,128)(2,1)}), bf16[512,256]{1,0:T(8,128)(2,1)}) %all-reduce.3.cloned.1.call-update) | async-done | bytes 262160 | tf_op jit(solution)/shard_map/psum | solution.py:41
  246.7 0.0 copy-done.1
  246.7 0.0 copy-done.4
  246.7 2.0 fusion.2
  248.7 0.0 all-gather.12.cloned.1.call-update
  248.7 0.0 all-reduce.5.cloned.1.call-start
  248.8 63.4 %all-gather.12.cloned.1.call-done = bf16[8192,256]{0,1:T(8,128)(2,1)} async-done(((bf16[512,256]{0,1:T(8,128)(2,1)}), bf16[8192,256]{0,1:T(8,128)(2,1)}) %all-gather.12.cloned.1.call-update) | async-done | bytes 4194320 | tf_op jit(solution)/shard_map/all_gather | solution.py:8
  312.2 4.0 copy.12
  316.2 2.5 bitcast_reduce_fusion
  318.8 1.0 fusion.3
  319.8 0.0 all-reduce.5.cloned.1.call-update
  319.8 0.0 reduce-scatter.9.cloned.1.call-start
  319.9 108.2 %all-reduce.5.cloned.1.call-done = bf16[512,256]{0,1:T(8,128)(2,1)} async-done(((bf16[512,256]{0,1:T(8,128)(2,1)}), bf16[512,256]{0,1:T(8,128)(2,1)}) %all-reduce.5.cloned.1.call-update) | async-done | bytes 262160 | tf_op jit(solution)/shard_map/psum | solution.py:45
  428.1 0.8 constant_dynamic-slice_fusion
  428.9 12.0 %all_gather.22 = bf16[512,256]{0,1:T(8,128)(2,1)S(1)} all-gather(bf16[128,256]{0,1:T(8,128)(2,1)S(1)} %constant_dynamic-slice_fusion), channel_id=1, replica_groups=mesh['leaf'=16,'row'=4,'col'=4] {'col'}, dimensions={0}, use_global_device_ids=true | all-gather | bytes 327680 | tf_op jit(solution)/shard_map/all_gather | solution.py:52
  440.9 0.0 copy-start.2
  440.9 1.7 fusion.1
  442.6 0.0 reduce-scatter.9.cloned.1.call-update
  442.6 0.0 all-gather.10.cloned.1.call-start
  442.7 23.6 %reduce-scatter.9.cloned.1.call-done = bf16[2048,64]{0,1:T(8,128)(2,1)} async-done(((bf16[2048,256]{0,1:T(8,128)(2,1)}), bf16[2048,64]{0,1:T(8,128)(2,1)}) %reduce-scatter.9.cloned.1.call-update) | async-done | bytes 262160 | tf_op jit(solution)/shard_map/reduce_scatter | solution.py:55
  466.3 0.0 copy-done.2
  466.3 1.7 subtract_convert_fusion
  468.0 0.0 all-gather.10.cloned.1.call-update
  468.0 0.0 copy-start.3
  468.0 0.0 reduce-scatter.11.cloned.1.call-start
  468.1 27.9 %all-gather.10.cloned.1.call-done = bf16[2048,256]{0,1:T(8,128)(2,1)} async-done(((bf16[2048,64]{0,1:T(8,128)(2,1)}), bf16[2048,256]{0,1:T(8,128)(2,1)}) %all-gather.10.cloned.1.call-update) | async-done | bytes 1048592 | tf_op jit(solution)/shard_map/all_gather | solution.py:59
  496.0 7.0 %fusion = bf16[2048,256]{0,1:T(8,128)(2,1)} fusion(bf16[2048,256]{0,1:T(8,128)(2,1)} %all-gather.10.cloned.1.call-done, bf16[2048,2048]{1,0:T(8,128)(2,1)} %param.8), kind=kOutput, calls=%fused_computation.3 | convolution fusion | flops 2148007936 | bytes 10485760 | tf_op jit(solution)/shard_map/dot_general | solution.py:13
  503.1 0.0 reduce-scatter.11.cloned.1.call-update
  503.1 0.0 copy-done.3
  503.1 0.9 copy.11
  504.0 26.5 %reduce-scatter.11.cloned.1.call-done = bf16[2048,64]{0,1:T(8,128)(2,1)} async-done(((bf16[2048,256]{0,1:T(8,128)(2,1)}), bf16[2048,64]{0,1:T(8,128)(2,1)}) %reduce-scatter.11.cloned.1.call-update) | async-done | bytes 262160 | tf_op jit(solution)/shard_map/reduce_scatter | solution.py:60
  530.5 1.8 convert_element_type.89
  (1 shorter events, 0.0 us)
Async XLA Ops:
  7.2 100.1 %copy-start = (bf16[2048,512]{1,0:T(8,128)(2,1)S(1)}, bf16[2048,512]{1,0:T(8,128)(2,1)}, u32[]{:S(2)}) copy-start(bf16[2048,512]{1,0:T(8,128)(2,1)} %param.9) | copy-start | bytes 6291460
  7.2 32.1 %all-gather.6.cloned.1.call-start = ((), (), s32[]{:S(2)}) async-start(), calls=%async_computation.4 | async-start | bytes 1310720 | tf_op jit(solution)/shard_map/all_gather | solution.py:24
  7.9 70.2 %reduce-scatter.5.cloned.1.call-start = ((), (), s32[]{:S(2)}) async-start(), calls=%async_computation.5 | async-start | bytes 2621440 | tf_op jit(solution)/shard_map/reduce_scatter | solution.py:27
  46.6 60.7 %all-gather.8.cloned.1.call-start = ((), (), s32[]{:S(2)}) async-start(), calls=%async_computation.6 | async-start | bytes 1310720 | tf_op jit(solution)/shard_map/all_gather | solution.py:30
  79.9 166.8 %copy-start.1 = (bf16[512,512]{1,0:T(8,128)(2,1)S(1)}, bf16[512,512]{1,0:T(8,128)(2,1)}, u32[]{:S(2)}) copy-start(bf16[512,512]{1,0:T(8,128)(2,1)} %param.10) | copy-start | bytes 1572868
  79.9 166.8 %copy-start.4 = (bf16[512,256]{1,0:T(8,128)(2,1)S(1)}, bf16[512,256]{1,0:T(8,128)(2,1)}, u32[]{:S(2)}) copy-start(bf16[512,256]{1,0:T(8,128)(2,1)} %param.7) | copy-start | bytes 786436
  79.9 55.7 %reduce-scatter.7.cloned.1.call-start = ((), (), s32[]{:S(2)}) async-start(), calls=%async_computation.7 | async-start | bytes 655360 | tf_op jit(solution)/shard_map/reduce_scatter | solution.py:31
  110.0 136.7 %all-reduce.3.cloned.1.call-start = ((), (), s32[]{:S(2)}) async-start(), calls=%async_computation.8 | async-start | bytes 524288 | tf_op jit(solution)/shard_map/psum | solution.py:41
  137.5 174.7 %all-gather.12.cloned.1.call-start = ((), (), s32[]{:S(2)}) async-start(), calls=%async_computation.13 | async-start | bytes 4456448 | tf_op jit(solution)/shard_map/all_gather | solution.py:8
  248.7 179.3 %all-reduce.5.cloned.1.call-start = ((), (), s32[]{:S(2)}) async-start(), calls=%async_computation.9 | async-start | bytes 524288 | tf_op jit(solution)/shard_map/psum | solution.py:45
  319.8 146.5 %reduce-scatter.9.cloned.1.call-start = ((), (), s32[]{:S(2)}) async-start(), calls=%async_computation.10 | async-start | bytes 1310720 | tf_op jit(solution)/shard_map/reduce_scatter | solution.py:55
  440.9 25.4 %copy-start.2 = (f32[2048,64]{0,1:T(8,128)S(1)}, f32[2048,64]{0,1:T(8,128)}, u32[]{:S(2)}) copy-start(f32[2048,64]{0,1:T(8,128)} %reduce-scatter.5.cloned.1.call-done) | copy-start | bytes 1572868
  442.6 53.4 %all-gather.10.cloned.1.call-start = ((), (), s32[]{:S(2)}) async-start(), calls=%async_computation.11 | async-start | bytes 1310720 | tf_op jit(solution)/shard_map/all_gather | solution.py:59
  468.0 35.1 %copy-start.3 = (bf16[512,256]{0,1:T(8,128)(2,1)S(1)}, bf16[512,256]{0,1:T(8,128)(2,1)}, u32[]{:S(2)}) copy-start(bf16[512,256]{0,1:T(8,128)(2,1)} %all-reduce.5.cloned.1.call-done) | copy-start | bytes 786436
  468.0 62.5 %reduce-scatter.11.cloned.1.call-start = ((), (), s32[]{:S(2)}) async-start(), calls=%async_computation.12 | async-start | bytes 1310720 | tf_op jit(solution)/shard_map/reduce_scatter | solution.py:60
Sparse Core Ops, SparseCore 0:
  9.8 29.3 all-gather.5
  46.7 31.3 reduce-scatter.4
  80.6 26.5 all-gather.7
  110.4 25.1 reduce-scatter.6
  138.4 108.2 all-reduce.2
  249.5 62.5 all-gather.11
  319.9 108.0 all-reduce.4
  442.8 23.4 reduce-scatter.8
  468.7 27.2 all-gather.9
  503.2 27.2 reduce-scatter.10
